TPU v7x, 32 devices: a whole 2x2x4 slice. The times are simulated.
32 devices in a mesh: tok: 4 (over y, core), voc: 8 (over z, x).
Axes of the slice: x: 2, y: 2, z: 4, core: 2. Of those that a mesh axis runs over, the one named last changes fastest.
Arguments:
- hidden: bfloat16 [1024, 2048], P('tok')
- panel: bfloat16 [2048, 8192], P(None, 'voc'), may hold values from -0.1875 to 0.1875
- in_proj: bfloat16 [2048, 64], replicated, may hold values from -0.125 to 0.125
- out_proj: bfloat16 [8192, 64], P('voc'), may hold values from -6 to 6
- targets: int32 [1024], P('tok'), may hold values from 0 to 8191
- keep: int32 [1024], P('tok'), may hold values 0 or 1
- span_ids: int32 [1024], P('tok'), may hold values from 0 to 127, as said below
- store: bfloat16 [8192, 4096], P(('tok', 'voc')), may hold values from -6 to 6
Outputs:
- hidden_grad: bfloat16 [1024, 2048], P('tok', 'voc')
- scores: float32 [128, 8192], P(None, ('tok', 'voc'))
Inputs may be any that keep to these rules, and one draw needn't show every extreme that they name: `span_ids`: tokens k * 256 to (k + 1) * 256 - 1 hold exactly the spans k * 32 to (k + 1) * 32 - 1 in increasing order, each of one or more tokens.
All inputs are finite; a program needn't handle non-finite values. No bound on the sum of `keep` on one device may be relied on, other than what follows from the above.
Results may differ from a plain program's by a relative error of at most 0.018.
Values may be sent and summed in bfloat16 or wider, within the bound.
A program may use at most 64 MiB of HBM per device.

v0:
```python
import jax
import jax.numpy as jnp
from jax import lax
from jax.sharding import PartitionSpec as P

RANK = 64
SPAN_DEV = 32


def span_sums(member, inner, outer):
    weighted = member[:, :, None] * inner[None, :, :]
    summed = lax.dot_general(
        weighted,
        outer,
        (((1,), (0,)), ((), ())),
        precision=lax.Precision.HIGHEST,
        preferred_element_type=jnp.float32,
    )
    return summed.reshape(member.shape[0], inner.shape[1] * outer.shape[1])


def body(hidden, panel, in_proj, out_proj, targets, keep, span_ids, store):
    panel_cols = panel.shape[1]
    logits = jnp.dot(hidden, panel, preferred_element_type=jnp.float32)
    local_top = jnp.max(logits, axis=1)
    top = lax.pmax(local_top, "voc")
    total = lax.psum(jnp.sum(jnp.exp(logits - top[:, None]), axis=1), "voc")
    lse = top + jnp.log(total)
    columns = lax.axis_index("voc") * panel_cols + jnp.arange(panel_cols, dtype=jnp.int32)
    onehot = (targets[:, None] == columns[None, :]).astype(jnp.float32)
    grad = ((jnp.exp(logits - lse[:, None]) - onehot) * keep.astype(jnp.float32)[:, None]).astype(
        jnp.bfloat16
    )
    partial_hidden = lax.dot_general(
        grad, panel, (((1,), (1,)), ((), ())), preferred_element_type=jnp.float32
    )
    hidden_grad = lax.psum_scatter(
        partial_hidden.astype(jnp.bfloat16), "voc", scatter_dimension=1, tiled=True
    )
    inner = jnp.dot(hidden, in_proj, preferred_element_type=jnp.float32)
    outer_part = jnp.dot(grad, out_proj, preferred_element_type=jnp.float32)
    local_span = span_ids - lax.axis_index("tok") * SPAN_DEV
    member = (local_span[None, :] == jnp.arange(SPAN_DEV, dtype=jnp.int32)[:, None]).astype(
        jnp.float32
    )
    outer = lax.psum(outer_part.astype(jnp.bfloat16), "voc").astype(jnp.float32)
    queries = span_sums(member, inner, outer).astype(jnp.bfloat16)
    scores = (
        lax.dot_general(
            lax.all_gather(queries, "tok", axis=0, tiled=True),
            store,
            (((1,), (1,)), ((), ())),
            preferred_element_type=jnp.float32,
        )
        / RANK
    )
    return (hidden_grad, scores)


def solution(mesh):
    placed = (
        P("tok", None),
        P(None, "voc"),
        P(),
        P("voc", None),
        P("tok"),
        P("tok"),
        P("tok"),
        P(("tok", "voc"), None),
    )
    return jax.shard_map(
        body,
        mesh=mesh,
        in_specs=placed,
        out_specs=(P("tok", "voc"), P(None, ("tok", "voc"))),
        check_vma=False,
    )
```

profile of v0, /device:TPU:0, one launch (start us, length us, event | category | flops | bytes accessed | tf_op | source)
XLA Modules:
  0.0 170.1 jit_solution(16016429621674106705)
XLA Ops:
  8.0 0.0 copy-start
  8.0 0.0 all-gather.2.cloned.1.call-start
  8.1 1.4 convert_element_type.30
  9.4 0.0 copy-start.3
  9.4 3.9 %fusion.9 = (f32[256]{0:T(256)S(1)}, f32[256,1024]{1,0:T(8,128)S(1)}) fusion(bf16[256,2048]{1,0:T(8,128)(2,1)} %param.8, bf16[2048,1024]{1,0:T(8,128)(2,1)} %param.9), kind=kOutput, calls=%fused_computation.16 | convolution fusion | flops 1074003712 | bytes 6292480 | tf_op jit(solution)/shard_map/dot_general | solution.py:24
  13.3 0.0 copy-start.4
  13.3 23.2 %pmax.7 = f32[256]{0:T(256)S(1)} all-reduce(f32[256]{0:T(256)S(1)} %get-tuple-element.2), channel_id=1, replica_groups=mesh['tok'=4,'voc'=8] {'voc'}, use_global_device_ids=true, to_apply=%region_1.0 | all-reduce | flops 256 | bytes 2048 | tf_op jit(solution)/shard_map/pmax | solution.py:26
  36.6 0.3 exponential_reduce_fusion
  36.9 17.1 %psum.14 = f32[256]{0:T(256)S(1)} all-reduce(f32[256]{0:T(256)S(1)} %exponential_reduce_fusion), channel_id=1, replica_groups=mesh['tok'=4,'voc'=8] {'voc'}, use_global_device_ids=true, to_apply=%region_3.0 | all-reduce | flops 256 | bytes 2048 | tf_op jit(solution)/shard_map/psum | solution.py:27
  54.0 0.0 copy-done.3
  54.0 2.3 %fusion.10 = f32[256,64]{0,1:T(8,128)} fusion(bf16[256,2048]{1,0:T(8,128)(2,1)} %param.8, bf16[2048,64]{0,1:T(8,128)(2,1)S(1)} %copy-done.3), kind=kOutput, calls=%fused_computation.17 | convolution fusion | flops 67108864 | bytes 1376256 | tf_op jit(solution)/shard_map/dot_general | solution.py:40
  56.3 0.0 copy-start.5
  56.3 0.7 broadcast_subtract_fusion
  57.0 1.0 multiply_convert_fusion
  58.1 0.0 copy-start.1
  58.1 0.8 copy-done.1
  58.9 0.0 copy-done.4
  58.9 0.3 convolution_convert_fusion.1
  59.2 0.0 copy-start.2
  59.2 35.0 %psum.15 = bf16[256,64]{0,1:T(8,128)(2,1)S(1)} all-reduce(bf16[256,64]{0,1:T(8,128)(2,1)S(1)} %convolution_convert_fusion.1), channel_id=1, replica_groups=mesh['tok'=4,'voc'=8] {'voc'}, use_global_device_ids=true, to_apply=%region_5.0 | all-reduce | flops 16384 | bytes 65536 | tf_op jit(solution)/shard_map/psum | solution.py:46
  94.2 0.0 copy-done.5
  94.2 1.1 fusion.2
  95.3 1.2 convert_element_type.36
  96.5 0.0 all-gather.2.cloned.1.call-update
  96.5 0.0 reduce-scatter.2.cloned.1.call-start
  96.6 0.0 copy-done.2
  96.6 4.5 %convolution_convert_fusion = bf16[256,2048]{1,0:T(8,128)(2,1)} fusion(bf16[256,1024]{1,0:T(8,128)(2,1)S(1)} %copy-done.2, bf16[2048,1024]{1,0:T(8,128)(2,1)} %param.9), kind=kOutput, calls=%fused_computation | convolution fusion | flops 1074266112 | bytes 5767168 | tf_op jit(solution)/shard_map/dot_general | solution.py:34
  101.1 0.0 reduce-scatter.2.cloned.1.call-update
  101.1 9.6 %all-gather.2.cloned.1.call-done = bf16[128,4096]{1,0:T(8,128)(2,1)} async-done(((bf16[32,4096]{1,0:T(8,128)(2,1)}), bf16[128,4096]{1,0:T(8,128)(2,1)}) %all-gather.2.cloned.1.call-update) | async-done | bytes 1048592 | tf_op jit(solution)/shard_map/all_gather | solution.py:50
  110.7 0.0 copy-done
  110.7 2.7 %convolution_multiply_fusion = f32[128,256]{1,0:T(8,128)} fusion(bf16[128,4096]{1,0:T(8,128)(2,1)} %all-gather.2.cloned.1.call-done, bf16[256,4096]{1,0:T(8,128)(2,1)S(1)} %copy-done), kind=kOutput, calls=%fused_computation.4 | convolution fusion | flops 268468224 | bytes 3276800 | tf_op jit(solution)/shard_map/dot_general | solution.py:49
  113.4 49.2 %reduce-scatter.2.cloned.1.call-done = bf16[256,256]{1,0:T(8,128)(2,1)} async-done(((bf16[256,2048]{1,0:T(8,128)(2,1)}), bf16[256,256]{1,0:T(8,128)(2,1)}) %reduce-scatter.2.cloned.1.call-update) | async-done | bytes 131088 | tf_op jit(solution)/shard_map/reduce_scatter | solution.py:37
  (3 shorter events, 0.0 us)
Async XLA Ops:
  8.0 102.7 %copy-start = (bf16[256,4096]{1,0:T(8,128)(2,1)S(1)}, bf16[256,4096]{1,0:T(8,128)(2,1)}, u32[]{:S(2)}) copy-start(bf16[256,4096]{1,0:T(8,128)(2,1)} %param.15) | copy-start | bytes 6291460
  8.0 102.7 %all-gather.2.cloned.1.call-start = ((), (), s32[]{:S(2)}) async-start(), calls=%async_computation.2 | async-start | bytes 1310720 | tf_op jit(solution)/shard_map/all_gather | solution.py:50
  9.4 44.6 %copy-start.3 = (bf16[2048,64]{0,1:T(8,128)(2,1)S(1)}, bf16[2048,64]{0,1:T(8,128)(2,1)}, u32[]{:S(2)}) copy-start(bf16[2048,64]{0,1:T(8,128)(2,1)} %param.10) | copy-start | bytes 786436
  13.3 45.6 %copy-start.4 = (bf16[1024,64]{0,1:T(8,128)(2,1)S(1)}, bf16[1024,64]{0,1:T(8,128)(2,1)}, u32[]{:S(2)}) copy-start(bf16[1024,64]{0,1:T(8,128)(2,1)} %param.11) | copy-start | bytes 393220
  56.3 37.9 %copy-start.5 = (f32[256,64]{0,1:T(8,128)S(1)}, f32[256,64]{0,1:T(8,128)}, u32[]{:S(2)}) copy-start(f32[256,64]{0,1:T(8,128)} %fusion.10) | copy-start | bytes 196612
  58.1 0.8 copy-start.1
  59.2 37.4 %copy-start.2 = (bf16[256,1024]{1,0:T(8,128)(2,1)S(1)}, bf16[256,1024]{1,0:T(8,128)(2,1)}, u32[]{:S(2)}) copy-start(bf16[256,1024]{1,0:T(8,128)(2,1)} %copy-done.1) | copy-start | bytes 1572868
  96.5 66.1 %reduce-scatter.2.cloned.1.call-start = ((), (), s32[]{:S(2)}) async-start(), calls=%async_computation.1 | async-start | bytes 1179648 | tf_op jit(solution)/shard_map/reduce_scatter | solution.py:37
Sparse Core Ops, SparseCore 0:
  96.6 14.0 all-gather.1
Sparse Core Ops, SparseCore 1:
  101.2 61.4 reduce-scatter.1
where the time goes:
time: 170 us
  blocking collectives  75.4 us (44%)
  waiting for transfers between devices  58.8 us (35%)
  between operations  15.5 us (9%)
  matrix products  14.8 us (9%)
  other arithmetic  3.44 us (2%)
  local copies, waits for them, and re-layouts  2.03 us (1%)
    reduce_scatter x1, waiting for transfers between devices, body(): lax.psum_scatter(partial_hidden.astype(jnp.bfloat16), 'voc', scatter_dime...  49.2 us
    psum x1, blocking collectives, body(): outer = lax.psum(outer_part.astype(jnp.bfloat16), 'voc').astype(jnp.float32)  35 us
    pmax x1, blocking collectives, body(): top = lax.pmax(local_top, 'voc')  23.2 us
    psum x1, blocking collectives, body(): total = lax.psum(jnp.sum(jnp.exp(logits - top[:, None]), axis=1), 'voc')  17.1 us
    all_gather x1, waiting for transfers between devices, body(): lax.all_gather(queries, 'tok', axis=0, tiled=True)  9.57 us
    dot_general x1, matrix products, body(): lax.dot_general(grad, panel, (((1,), (1,)), ((), ())), preferred_element_...  4.51 us
    dot_general x1, matrix products, body(): logits = jnp.dot(hidden, panel, preferred_element_type=jnp.float32)  3.88 us
  transfers between devices with their start and end apart: 2, of which 2 were waited for; matrix products, arithmetic and copies ran while one was open for 4% of the time, Pallas kernels for 0%

commit v1 on v0

--- a/solution.py
+++ b/solution.py
@@ -1,10 +1,17 @@
+import functools
+
 import jax
 import jax.numpy as jnp
 from jax import lax
+from jax.experimental import pallas as pl
+from jax.experimental.pallas import tpu as pltpu
 from jax.sharding import PartitionSpec as P
 
-RANK = 64
 SPAN_DEV = 32
+LANES = 128
+ROWS16 = 16
+PAIR = 2
+MESH_ID = pl.DeviceIdType.MESH
 
 
 def span_sums(member, inner, outer):
@@ -19,7 +26,7 @@
     return summed.reshape(member.shape[0], inner.shape[1] * outer.shape[1])
 
 
-def body(hidden, panel, in_proj, out_proj, targets, keep, span_ids, store):
+def plain_body(hidden, panel, in_proj, out_proj, targets, keep, span_ids, store):
     panel_cols = panel.shape[1]
     logits = jnp.dot(hidden, panel, preferred_element_type=jnp.float32)
     local_top = jnp.max(logits, axis=1)
@@ -52,9 +59,366 @@
             (((1,), (1,)), ((), ())),
             preferred_element_type=jnp.float32,
         )
-        / RANK
+        / in_proj.shape[1]
     )
     return (hidden_grad, scores)
+
+
+def dot_nt(a, b):
+    return lax.dot_general(a, b, (((1,), (1,)), ((), ())), preferred_element_type=jnp.float32)
+
+
+def fused_kernel(
+    n_tok,
+    n_voc,
+    chunks,
+    hidden_hbm,
+    panel_hbm,
+    inp_hbm,
+    outp_hbm,
+    targets_ref,
+    keep_ref,
+    span_ref,
+    store_hbm,
+    hg_ref,
+    scores_ref,
+    hidden,
+    panel,
+    inp,
+    outp,
+    store,
+    logits,
+    colstat,
+    both,
+    prod,
+    stat,
+    early,
+    opart,
+    rs,
+    oall,
+    weights,
+    queries,
+    xsrc,
+    xdst,
+    zsrc,
+    zdst,
+    load_sem,
+    panel_sem,
+    stat_s,
+    stat_r,
+    early_s,
+    early_r,
+    rs_s,
+    rs_r,
+    ag_s,
+    ag_r,
+    late_s,
+    late_r,
+    x_s,
+    x_r,
+    z_s,
+    z_r,
+):
+    tok, dim = hidden.shape
+    cols = panel.shape[1]
+    rank = inp.shape[1]
+    out_cols = dim // n_voc
+    nz = n_voc // PAIR
+    halves = tok // LANES
+    i = lax.axis_index("tok")
+    v = lax.axis_index("voc")
+    z, x = v // PAIR, v % PAIR
+    vpeers = [lax.rem(v + k, n_voc) for k in range(1, n_voc)]
+    tpeers = [lax.rem(i + k, n_tok) for k in range(1, n_tok)]
+    partner = z * PAIR + (PAIR - 1 - x)
+
+    def remote(src, dst, ss, rs_, t, w):
+        return pltpu.make_async_remote_copy(
+            src_ref=src,
+            dst_ref=dst,
+            send_sem=ss,
+            recv_sem=rs_,
+            device_id=(t, w),
+            device_id_type=MESH_ID,
+        )
+
+    barrier = pltpu.get_barrier_semaphore()
+    for w in vpeers:
+        pl.semaphore_signal(barrier, inc=1, device_id=(i, w), device_id_type=MESH_ID)
+    for t in tpeers:
+        pl.semaphore_signal(barrier, inc=1, device_id=(t, v), device_id_type=MESH_ID)
+
+    width = cols // chunks
+    load_hidden = pltpu.make_async_copy(hidden_hbm, hidden, load_sem.at[0])
+    load_hidden.start()
+    load_inp = pltpu.make_async_copy(inp_hbm, inp, load_sem.at[1])
+    load_inp.start()
+    load_panel = []
+    for c in range(chunks):
+        piece = pl.ds(c * width, width)
+        load_panel.append(
+            pltpu.make_async_copy(panel_hbm.at[:, piece], panel.at[:, piece], panel_sem.at[c])
+        )
+        load_panel[-1].start()
+    load_outp = pltpu.make_async_copy(outp_hbm, outp, load_sem.at[2])
+    load_outp.start()
+    load_store = pltpu.make_async_copy(store_hbm, store, load_sem.at[3])
+    load_store.start()
+
+    target_col = jnp.broadcast_to(targets_ref[...].astype(jnp.float32), (LANES, tok)).T
+    keep_row = keep_ref[...].astype(jnp.float32)
+    keep_col = jnp.broadcast_to(keep_row, (LANES, tok)).T
+    first = (v * cols).astype(jnp.float32)
+    colstat[1] = target_col - first
+    colstat[2] = keep_col
+
+    load_hidden.wait()
+    load_inp.wait()
+    inner = jnp.dot(hidden[...], inp[...], preferred_element_type=jnp.float32)
+    early[i, 0:rank, :] = inner.T.astype(jnp.bfloat16)
+    local_span = (span_ref[...] - i * SPAN_DEV).astype(jnp.float32)
+    early[i, rank : rank + ROWS16, :] = jnp.broadcast_to(local_span, (ROWS16, tok)).astype(
+        jnp.bfloat16
+    )
+
+    for c in range(chunks):
+        load_panel[c].wait()
+        piece = pl.ds(c * width, width)
+        logits[:, piece] = jnp.dot(hidden[...], panel[:, piece], preferred_element_type=jnp.float32)
+
+    step = 32
+    lane = lax.broadcasted_iota(jnp.int32, (step, LANES), 1)
+    number = lax.broadcasted_iota(jnp.int32, (step, cols), 1).astype(jnp.float32)
+
+    @pl.loop(0, tok // step)
+    def _(r):
+        at = pl.ds(pl.multiple_of(r * step, step), step)
+        l = logits[at, :]
+        m = jnp.max(l, axis=1, keepdims=True)
+        e = jnp.exp(l - m)
+        s = jnp.sum(e, axis=1, keepdims=True)
+        colstat[0, at, :] = jnp.where(lane == 0, m, s)
+        both[at, :] = e.astype(jnp.bfloat16)
+        hit = number == colstat[1, at, 0:1]
+        lower = pl.ds(pl.multiple_of(tok + r * step, step), step)
+        both[lower, :] = jnp.where(hit, colstat[2, at, 0:1], 0.0).astype(jnp.bfloat16)
+
+    mine = colstat[0].T[0:8, :]
+    stat[v] = mine
+
+    pl.semaphore_wait(barrier, n_voc + n_tok - 2)
+    sends = []
+
+    def send(copy):
+        copy.start()
+        sends.append(copy)
+
+    for k, w in enumerate(vpeers):
+        send(remote(stat.at[v], stat.at[v], stat_s.at[k], stat_r.at[v], i, w))
+    for k, t in enumerate(tpeers):
+        send(remote(early.at[i], early.at[i], early_s.at[k], early_r.at[i], t, v))
+
+    load_outp.wait()
+    outer2 = jnp.dot(both[...], outp[...], preferred_element_type=jnp.float32)
+
+    @pl.loop(0, n_voc)
+    def _(d):
+        at = pl.ds(pl.multiple_of(d * out_cols, out_cols), out_cols)
+        prod[d] = dot_nt(both[...], panel[at, :])
+
+    for k, w in enumerate(vpeers):
+        remote(stat.at[v], stat.at[w], stat_s.at[k], stat_r.at[w], i, w).wait_recv()
+    tops = [stat[w, 0:1, :] for w in range(n_voc)]
+    top = functools.reduce(jnp.maximum, tops)
+    total = functools.reduce(
+        jnp.add, [stat[w, 1:2, :] * jnp.exp(tops[w] - top) for w in range(n_voc)]
+    )
+    lse = top + jnp.log(total)
+    factor = keep_row * jnp.exp(mine[0:1, :] - lse)
+    colstat[3] = jnp.broadcast_to(factor, (LANES, tok)).T
+    factor_col = colstat[3, :, 0:1]
+
+    outer_t = (factor_col * outer2[:tok] - outer2[tok:]).T.astype(jnp.bfloat16)
+    for j in range(n_voc):
+        a, h = j // halves, j % halves
+        opart[j] = outer_t[a * ROWS16 : (a + 1) * ROWS16, h * LANES : (h + 1) * LANES]
+    for k, w in enumerate(vpeers):
+        send(remote(opart.at[w], rs.at[v], rs_s.at[k], rs_r.at[v], i, w))
+
+    def part_of(d):
+        return factor_col * prod[d, 0:tok, :] - prod[d, tok : 2 * tok, :]
+
+    order = [lax.rem(z + k, nz) for k in list(range(1, nz)) + [0]]
+    for k, zz in enumerate(order):
+        xsrc[k] = part_of(zz * PAIR + (PAIR - 1 - x)).astype(jnp.bfloat16)
+        send(remote(xsrc.at[k], xdst.at[k], x_s.at[k], x_r.at[k], i, partner))
+
+    for k, w in enumerate(vpeers):
+        remote(opart.at[w], rs.at[w], rs_s.at[k], rs_r.at[w], i, w).wait_recv()
+    rs[v] = opart[v]
+    outer_mine = functools.reduce(jnp.add, [rs[w].astype(jnp.float32) for w in range(n_voc)])
+    oall[i, v] = outer_mine.astype(jnp.bfloat16)
+    for k, w in enumerate(vpeers):
+        send(remote(oall.at[i, v], oall.at[i, v], ag_s.at[k], ag_r.at[v], i, w))
+
+    def pass_on(k):
+        zz = order[k]
+        remote(xsrc.at[k], xdst.at[k], x_s.at[k], x_r.at[k], i, partner).wait_recv()
+        total_k = part_of(zz * PAIR + x) + xdst[k].astype(jnp.float32)
+        if k == nz - 1:
+            return total_k
+        zsrc[k] = total_k.astype(jnp.bfloat16)
+        send(remote(zsrc.at[k], zdst.at[z], z_s.at[k], z_r.at[z], i, zz * PAIR + x))
+
+    pass_on(0)
+    for k, w in enumerate(vpeers):
+        remote(oall.at[i, v], oall.at[i, w], ag_s.at[k], ag_r.at[w], i, w).wait_recv()
+    for k, t in enumerate(tpeers):
+        send(remote(oall.at[i], oall.at[i], late_s.at[k], late_r.at[i], t, v))
+    for k in range(1, nz - 1):
+        pass_on(k)
+
+    for k, t in enumerate(tpeers):
+        remote(early.at[i], early.at[t], early_s.at[k], early_r.at[t], t, v).wait_recv()
+    span_no = lax.broadcasted_iota(jnp.int32, (SPAN_DEV, tok), 0).astype(jnp.float32)
+
+    @pl.loop(0, n_tok)
+    def _(b):
+        ids = early[b, rank : rank + ROWS16, :].astype(jnp.float32)[0:1]
+        member = (span_no == ids).astype(jnp.float32)
+        inner_t = early[b, 0:rank, :].astype(jnp.float32)
+        for a in range(rank):
+            weights[b, a * SPAN_DEV : (a + 1) * SPAN_DEV, :] = (
+                member * inner_t[a : a + 1, :]
+            ).astype(jnp.bfloat16)
+
+    kept = pass_on(nz - 1)
+    hold = prod.at[0, 0:tok, :]
+    hold[...] = kept
+
+    for k, t in enumerate(tpeers):
+        remote(oall.at[i], oall.at[t], late_s.at[k], late_r.at[t], t, v).wait_recv()
+    low = lax.broadcasted_iota(jnp.int32, (SPAN_DEV, LANES), 1) < rank
+
+    @pl.loop(0, n_tok)
+    def _(b):
+        rows = []
+        for a in range(rank // ROWS16):
+            rows.append(
+                jnp.concatenate([oall[b, a * halves + h] for h in range(halves)], axis=1)
+            )
+        outer_b = jnp.concatenate(rows * (LANES // rank), axis=0)
+        sums = dot_nt(weights[b], outer_b)
+        at = pl.ds(pl.multiple_of(b * SPAN_DEV, SPAN_DEV), SPAN_DEV)
+        for a in range(0, rank, 2):
+            even = sums[a * SPAN_DEV : (a + 1) * SPAN_DEV]
+            odd = sums[(a + 1) * SPAN_DEV : (a + 2) * SPAN_DEV]
+            queries[at, a * rank : (a + 2) * rank] = jnp.where(low, even, odd).astype(
+                jnp.bfloat16
+            )
+
+    load_store.wait()
+    scores_ref[...] = dot_nt(queries[...], store[...]) / rank
+
+    for k in range(1, nz):
+        w = lax.rem(z + k, nz)
+        remote(zsrc.at[0], zdst.at[w], z_s.at[0], z_r.at[w], i, w * PAIR + x).wait_recv()
+    zdst[z] = jnp.zeros_like(zdst[z])
+    hg_ref[...] = (
+        hold[...]
+        + functools.reduce(jnp.add, [zdst[w].astype(jnp.float32) for w in range(nz)])
+    ).astype(jnp.bfloat16)
+    for copy in sends:
+        copy.wait_send()
+
+
+def fused_fits(n_tok, n_voc, hidden, panel, in_proj):
+    tok, dim = hidden.shape
+    rank = in_proj.shape[1]
+    return (
+        n_voc % PAIR == 0
+        and n_tok > 1
+        and (rank // ROWS16) * (tok // LANES) == n_voc
+        and rank * 2 == LANES
+        and dim % (n_voc * LANES) == 0
+        and panel.shape[1] % (2 * LANES) == 0
+        and SPAN_DEV % ROWS16 == 0
+    )
+
+
+def body(n_tok, n_voc, hidden, panel, in_proj, out_proj, targets, keep, span_ids, store):
+    if not fused_fits(n_tok, n_voc, hidden, panel, in_proj):
+        return plain_body(hidden, panel, in_proj, out_proj, targets, keep, span_ids, store)
+    tok, dim = hidden.shape
+    cols = panel.shape[1]
+    rank = in_proj.shape[1]
+    out_cols = dim // n_voc
+    nz = n_voc // PAIR
+    chunks = cols // (2 * LANES)
+    bf, f32 = jnp.bfloat16, jnp.float32
+    block = (nz, tok, out_cols)
+    dma = pltpu.SemaphoreType.DMA
+    anywhere = pl.BlockSpec(memory_space=pl.ANY)
+    vmem = pl.BlockSpec(memory_space=pltpu.VMEM)
+    return pl.pallas_call(
+        functools.partial(fused_kernel, n_tok, n_voc, chunks),
+        out_shape=(
+            jax.ShapeDtypeStruct((tok, out_cols), bf),
+            jax.ShapeDtypeStruct((n_tok * SPAN_DEV, store.shape[0]), f32),
+        ),
+        in_specs=[anywhere] * 4 + [vmem] * 3 + [anywhere],
+        out_specs=(vmem, vmem),
+        scratch_shapes=[
+            pltpu.VMEM(hidden.shape, bf),
+            pltpu.VMEM(panel.shape, bf),
+            pltpu.VMEM(in_proj.shape, bf),
+            pltpu.VMEM(out_proj.shape, bf),
+            pltpu.VMEM(store.shape, bf),
+            pltpu.VMEM((tok, cols), f32),
+            pltpu.VMEM((4, tok, LANES), f32),
+            pltpu.VMEM((2 * tok, cols), bf),
+            pltpu.VMEM((n_voc, 2 * tok, out_cols), f32),
+            pltpu.VMEM((n_voc, 8, tok), f32),
+            pltpu.VMEM((n_tok, rank + ROWS16, tok), bf),
+            pltpu.VMEM((n_voc, ROWS16, LANES), bf),
+            pltpu.VMEM((n_voc, ROWS16, LANES), bf),
+            pltpu.VMEM((n_tok, n_voc, ROWS16, LANES), bf),
+            pltpu.VMEM((n_tok, rank * SPAN_DEV, tok), bf),
+            pltpu.VMEM((n_tok * SPAN_DEV, rank * rank), bf),
+            pltpu.VMEM(block, bf),
+            pltpu.VMEM(block, bf),
+            pltpu.VMEM(block, bf),
+            pltpu.VMEM(block, bf),
+            dma((4,)),
+            dma((chunks,)),
+            dma((n_voc,)),
+            dma((n_voc,)),
+            dma((n_tok,)),
+            dma((n_tok,)),
+            dma((n_voc,)),
+            dma((n_voc,)),
+            dma((n_voc,)),
+            dma((n_voc,)),
+            dma((n_tok,)),
+            dma((n_tok,)),
+            dma((nz,)),
+            dma((nz,)),
+            dma((nz,)),
+            dma((nz,)),
+        ],
+        compiler_params=pltpu.CompilerParams(
+            collective_id=0, has_side_effects=True, vmem_limit_bytes=44 * 1024 * 1024
+        ),
+    )(
+        hidden,
+        panel,
+        in_proj,
+        out_proj,
+        targets.reshape(1, tok),
+        keep.reshape(1, tok),
+        span_ids.reshape(1, tok),
+        store,
+    )
 
 
 def solution(mesh):
@@ -69,7 +433,7 @@
         P(("tok", "voc"), None),
     )
     return jax.shard_map(
-        body,
+        functools.partial(body, mesh.shape["tok"], mesh.shape["voc"]),
         mesh=mesh,
         in_specs=placed,
         out_specs=(P("tok", "voc"), P(None, ("tok", "voc"))),

time: 170 us -> 48.7 us (0.29)
  blocking collectives: 75.4 us -> 0 us
  waiting for transfers between devices: 58.8 us -> 0 us
  Pallas kernels: 0 us -> 37.1 us
  between operations: 15.5 us -> 0.67 us
  matrix products: 14.8 us -> 0 us
  local copies, waits for them, and re-layouts: 2.03 us -> 10.6 us
  other arithmetic: 3.44 us -> 0 us
    psum x2 -> x0, blocking collectives: 52.1 us -> none  [the longest x1 35 us: body(): outer = lax.psum(outer_part.astype(jnp.bfloat16), 'voc').astype(jnp.float32)]
    reduce_scatter x1 -> x0, waiting for transfers between devices: 49.2 us -> none  [body(): lax.psum_scatter(partial_hidden.astype(jnp.bfloat16), 'voc', scatter_dime...]
    pallas_call x0 -> x1, Pallas kernels: none -> 37.1 us  [body(): pl.pallas_call(functools.partial(fused_kernel, n_tok, n_voc, chunks), out...]
    pmax x1 -> x0, blocking collectives: 23.2 us -> none  [body(): top = lax.pmax(local_top, 'voc')]
    dot_general x6 -> x0, matrix products: 14.8 us -> none  [the longest x1 4.51 us: body(): lax.dot_general(grad, panel, (((1,), (1,)), ((), ())), preferred_element_...]
    unnamed x12 -> x16, local copies, waits for them, and re-layouts: 0.84 us -> 10.6 us
    all_gather x1 -> x0, waiting for transfers between devices: 9.57 us -> none  [body(): lax.all_gather(queries, 'tok', axis=0, tiled=True)]
    convert_element_type x3 -> x0, other arithmetic: 2.42 us -> none  [the longest x1 1.38 us: body(): keep.astype(jnp.float32)[:, None]]
  transfers between devices with their start and end apart: 2 -> 0, of which waited for: 2 -> 0; matrix products, arithmetic and copies ran while one was open for 4% -> 0% of each run, Pallas kernels for 0% -> 0%
where the time goes in v1:
time: 48.7 us; the launch traced here: 48.4 us
  Pallas kernels  37.1 us (76%)
  local copies, waits for them, and re-layouts  10.6 us (22%)
  between operations  0.67 us (1%)
    pallas_call x1, Pallas kernels, body(): pl.pallas_call(functools.partial(fused_kernel, n_tok, n_voc, chunks), out...  37.1 us
    unnamed x16, local copies, waits for them, and re-layouts  10.6 us

profile of v1, /device:TPU:0, one launch (start us, length us, event | category | flops | bytes accessed | tf_op | source)
XLA Modules:
  0.0 48.4 jit_solution(11304664877250477465)
XLA Ops:
  0.6 1.1 %copy.11.outp_hbm = bf16[1024,64]{1,0:T(8,128)(2,1)S(1)} copy(bf16[1024,64]{0,1:T(8,128)(2,1)} %param.11) | data formatting | bytes 262144 | tf_op args[3]
  1.7 1.2 %copy.10.inp_hbm = bf16[2048,64]{1,0:T(8,128)(2,1)S(1)} copy(bf16[2048,64]{0,1:T(8,128)(2,1)} %param.10) | data formatting | bytes 524288 | tf_op args[2]
  2.9 0.0 copy-start
  3.0 2.2 %copy-done = bf16[2048,1024]{1,0:T(8,128)(2,1)S(1)} copy-done((bf16[2048,1024]{1,0:T(8,128)(2,1)S(1)}, bf16[2048,1024]{1,0:T(8,128)(2,1)}, u32[]{:S(2)}) %copy-start) | copy-done | bytes 4194328
  5.1 0.0 copy-start.1
  5.1 1.6 %copy-done.1 = bf16[256,4096]{1,0:T(8,128)(2,1)S(1)} copy-done((bf16[256,4096]{1,0:T(8,128)(2,1)S(1)}, bf16[256,4096]{1,0:T(8,128)(2,1)}, u32[]{:S(2)}) %copy-start.1) | copy-done | bytes 2097176
  6.7 0.0 copy-start.2
  6.7 1.2 %copy-done.2 = bf16[256,2048]{1,0:T(8,128)(2,1)S(1)} copy-done((bf16[256,2048]{1,0:T(8,128)(2,1)S(1)}, bf16[256,2048]{1,0:T(8,128)(2,1)}, u32[]{:S(2)}) %copy-start.2) | copy-done | bytes 1048600
  8.0 0.0 copy-start.3
  8.0 0.7 %copy-done.3 = s32[256]{0:T(256)S(1)} copy-done((s32[256]{0:T(256)S(1)}, s32[256]{0:T(256)}, u32[]{:S(2)}) %copy-start.3) | copy-done | bytes 1048
  8.6 0.0 copy-start.4
  8.6 0.7 %copy-done.4 = s32[256]{0:T(256)S(1)} copy-done((s32[256]{0:T(256)S(1)}, s32[256]{0:T(256)}, u32[]{:S(2)}) %copy-start.4) | copy-done | bytes 1048
  9.3 0.0 copy-start.5
  9.3 0.7 %copy-done.5 = s32[256]{0:T(256)S(1)} copy-done((s32[256]{0:T(256)S(1)}, s32[256]{0:T(256)}, u32[]{:S(2)}) %copy-start.5) | copy-done | bytes 1048
  10.0 37.1 %shard_map.95 = (bf16[256,256]{1,0:T(8,128)(2,1)S(1)}, f32[128,256]{1,0:T(8,128)S(1)}) custom-call(bf16[256,2048]{1,0:T(8,128)(2,1)S(1)} %copy-done.2, bf16[2048,1024]{1,0:T(8,128)(2,1)S(1)} %copy-done, bf16[2048,64]{1,0:T(8,128)(2,1)S(1)} %copy.10.inp_hbm, bf16[1024,64]{1,0:T(8,128)(2,1)S(1)} %copy.11.outp_hbm, s32[1,256]{1,0:T(1,128)S(1)} %bitcast.3, ...), custom_call_target="tpu_custom_call" | custom-call | tf_op jit(solution)/shard_map/pallas_call | solution.py:363
  47.1 0.7 %copy.14 = bf16[256,256]{1,0:T(8,128)(2,1)} copy(bf16[256,256]{1,0:T(8,128)(2,1)S(1)} %get-tuple-element.4) | data formatting | bytes 262144
  47.7 0.7 %copy.15 = f32[128,256]{1,0:T(8,128)} copy(f32[128,256]{1,0:T(8,128)S(1)} %get-tuple-element.5) | data formatting | bytes 262144
Async XLA Ops:
  2.9 2.2 %copy-start = (bf16[2048,1024]{1,0:T(8,128)(2,1)S(1)}, bf16[2048,1024]{1,0:T(8,128)(2,1)}, u32[]{:S(2)}) copy-start(bf16[2048,1024]{1,0:T(8,128)(2,1)} %panel_hbm.1) | copy-start | bytes 12582916
  5.1 1.6 %copy-start.1 = (bf16[256,4096]{1,0:T(8,128)(2,1)S(1)}, bf16[256,4096]{1,0:T(8,128)(2,1)}, u32[]{:S(2)}) copy-start(bf16[256,4096]{1,0:T(8,128)(2,1)} %store_hbm.1) | copy-start | bytes 6291460
  6.7 1.2 %copy-start.2 = (bf16[256,2048]{1,0:T(8,128)(2,1)S(1)}, bf16[256,2048]{1,0:T(8,128)(2,1)}, u32[]{:S(2)}) copy-start(bf16[256,2048]{1,0:T(8,128)(2,1)} %hidden_hbm.1) | copy-start | bytes 3145732
  8.0 0.7 %copy-start.3 = (s32[256]{0:T(256)S(1)}, s32[256]{0:T(256)}, u32[]{:S(2)}) copy-start(s32[256]{0:T(256)} %param.12) | copy-start | bytes 3076
  8.6 0.7 %copy-start.4 = (s32[256]{0:T(256)S(1)}, s32[256]{0:T(256)}, u32[]{:S(2)}) copy-start(s32[256]{0:T(256)} %param.13) | copy-start | bytes 3076
  9.3 0.7 %copy-start.5 = (s32[256]{0:T(256)S(1)}, s32[256]{0:T(256)}, u32[]{:S(2)}) copy-start(s32[256]{0:T(256)} %param.14) | copy-start | bytes 3076

commit v2 on v1

--- a/solution.py
+++ b/solution.py
@@ -76,9 +76,9 @@
     panel_hbm,
     inp_hbm,
     outp_hbm,
-    targets_ref,
-    keep_ref,
-    span_ref,
+    targets_hbm,
+    keep_hbm,
+    span_hbm,
     store_hbm,
     hg_ref,
     scores_ref,
@@ -87,6 +87,7 @@
     inp,
     outp,
     store,
+    ids_ref,
     logits,
     colstat,
     both,
@@ -121,7 +122,7 @@
 ):
     tok, dim = hidden.shape
     cols = panel.shape[1]
-    rank = inp.shape[1]
+    rank = inp.shape[0]
     out_cols = dim // n_voc
     nz = n_voc // PAIR
     halves = tok // LANES
@@ -149,6 +150,10 @@
         pl.semaphore_signal(barrier, inc=1, device_id=(t, v), device_id_type=MESH_ID)
 
     width = cols // chunks
+    loads = []
+    for k, ref in enumerate((targets_hbm, keep_hbm, span_hbm)):
+        loads.append(pltpu.make_async_copy(ref, ids_ref.at[k], load_sem.at[4 + k]))
+        loads[-1].start()
     load_hidden = pltpu.make_async_copy(hidden_hbm, hidden, load_sem.at[0])
     load_hidden.start()
     load_inp = pltpu.make_async_copy(inp_hbm, inp, load_sem.at[1])
@@ -165,8 +170,10 @@
     load_store = pltpu.make_async_copy(store_hbm, store, load_sem.at[3])
     load_store.start()
 
-    target_col = jnp.broadcast_to(targets_ref[...].astype(jnp.float32), (LANES, tok)).T
-    keep_row = keep_ref[...].astype(jnp.float32)
+    for copy in loads:
+        copy.wait()
+    target_col = jnp.broadcast_to(ids_ref[0].astype(jnp.float32), (LANES, tok)).T
+    keep_row = ids_ref[1].astype(jnp.float32)
     keep_col = jnp.broadcast_to(keep_row, (LANES, tok)).T
     first = (v * cols).astype(jnp.float32)
     colstat[1] = target_col - first
@@ -174,9 +181,8 @@
 
     load_hidden.wait()
     load_inp.wait()
-    inner = jnp.dot(hidden[...], inp[...], preferred_element_type=jnp.float32)
-    early[i, 0:rank, :] = inner.T.astype(jnp.bfloat16)
-    local_span = (span_ref[...] - i * SPAN_DEV).astype(jnp.float32)
+    early[i, 0:rank, :] = dot_nt(inp[...], hidden[...]).astype(jnp.bfloat16)
+    local_span = (ids_ref[2] - i * SPAN_DEV).astype(jnp.float32)
     early[i, rank : rank + ROWS16, :] = jnp.broadcast_to(local_span, (ROWS16, tok)).astype(
         jnp.bfloat16
     )
@@ -219,7 +225,7 @@
         send(remote(early.at[i], early.at[i], early_s.at[k], early_r.at[i], t, v))
 
     load_outp.wait()
-    outer2 = jnp.dot(both[...], outp[...], preferred_element_type=jnp.float32)
+    outer2 = dot_nt(outp[...], both[...])
 
     @pl.loop(0, n_voc)
     def _(d):
@@ -238,7 +244,7 @@
     colstat[3] = jnp.broadcast_to(factor, (LANES, tok)).T
     factor_col = colstat[3, :, 0:1]
 
-    outer_t = (factor_col * outer2[:tok] - outer2[tok:]).T.astype(jnp.bfloat16)
+    outer_t = (factor * outer2[:, :tok] - outer2[:, tok:]).astype(jnp.bfloat16)
     for j in range(n_voc):
         a, h = j // halves, j % halves
         opart[j] = outer_t[a * ROWS16 : (a + 1) * ROWS16, h * LANES : (h + 1) * LANES]
@@ -248,18 +254,12 @@
     def part_of(d):
         return factor_col * prod[d, 0:tok, :] - prod[d, tok : 2 * tok, :]
 
-    order = [lax.rem(z + k, nz) for k in list(range(1, nz)) + [0]]
-    for k, zz in enumerate(order):
-        xsrc[k] = part_of(zz * PAIR + (PAIR - 1 - x)).astype(jnp.bfloat16)
+    shifts = [nz // 2] + [k for k in range(1, nz) if k != nz // 2] + [0]
+    order = [lax.rem(z + k, nz) for k in shifts]
+
+    def send_x(k):
+        xsrc[k] = part_of(order[k] * PAIR + (PAIR - 1 - x)).astype(jnp.bfloat16)
         send(remote(xsrc.at[k], xdst.at[k], x_s.at[k], x_r.at[k], i, partner))
-
-    for k, w in enumerate(vpeers):
-        remote(opart.at[w], rs.at[w], rs_s.at[k], rs_r.at[w], i, w).wait_recv()
-    rs[v] = opart[v]
-    outer_mine = functools.reduce(jnp.add, [rs[w].astype(jnp.float32) for w in range(n_voc)])
-    oall[i, v] = outer_mine.astype(jnp.bfloat16)
-    for k, w in enumerate(vpeers):
-        send(remote(oall.at[i, v], oall.at[i, v], ag_s.at[k], ag_r.at[v], i, w))
 
     def pass_on(k):
         zz = order[k]
@@ -270,14 +270,7 @@
         zsrc[k] = total_k.astype(jnp.bfloat16)
         send(remote(zsrc.at[k], zdst.at[z], z_s.at[k], z_r.at[z], i, zz * PAIR + x))
 
-    pass_on(0)
-    for k, w in enumerate(vpeers):
-        remote(oall.at[i, v], oall.at[i, w], ag_s.at[k], ag_r.at[w], i, w).wait_recv()
-    for k, t in enumerate(tpeers):
-        send(remote(oall.at[i], oall.at[i], late_s.at[k], late_r.at[i], t, v))
-    for k in range(1, nz - 1):
-        pass_on(k)
-
+    send_x(0)
     for k, t in enumerate(tpeers):
         remote(early.at[i], early.at[t], early_s.at[k], early_r.at[t], t, v).wait_recv()
     span_no = lax.broadcasted_iota(jnp.int32, (SPAN_DEV, tok), 0).astype(jnp.float32)
@@ -292,9 +285,22 @@
                 member * inner_t[a : a + 1, :]
             ).astype(jnp.bfloat16)
 
-    kept = pass_on(nz - 1)
-    hold = prod.at[0, 0:tok, :]
-    hold[...] = kept
+    for k, w in enumerate(vpeers):
+        remote(opart.at[w], rs.at[w], rs_s.at[k], rs_r.at[w], i, w).wait_recv()
+    rs[v] = opart[v]
+    outer_mine = functools.reduce(jnp.add, [rs[w].astype(jnp.float32) for w in range(n_voc)])
+    oall[i, v] = outer_mine.astype(jnp.bfloat16)
+    for k, w in enumerate(vpeers):
+        send(remote(oall.at[i, v], oall.at[i, v], ag_s.at[k], ag_r.at[v], i, w))
+    for k in range(1, nz):
+        send_x(k)
+    pass_on(0)
+
+    for k, w in enumerate(vpeers):
+        remote(oall.at[i, v], oall.at[i, w], ag_s.at[k], ag_r.at[w], i, w).wait_recv()
+    for k, t in enumerate(tpeers):
+        send(remote(oall.at[i], oall.at[i], late_s.at[k], late_r.at[i], t, v))
+    pass_on(1)
 
     for k, t in enumerate(tpeers):
         remote(oall.at[i], oall.at[t], late_s.at[k], late_r.at[t], t, v).wait_recv()
@@ -317,15 +323,18 @@
                 jnp.bfloat16
             )
 
+    for k in range(2, nz - 1):
+        pass_on(k)
     load_store.wait()
     scores_ref[...] = dot_nt(queries[...], store[...]) / rank
 
+    kept = pass_on(nz - 1)
     for k in range(1, nz):
         w = lax.rem(z + k, nz)
         remote(zsrc.at[0], zdst.at[w], z_s.at[0], z_r.at[w], i, w * PAIR + x).wait_recv()
     zdst[z] = jnp.zeros_like(zdst[z])
     hg_ref[...] = (
-        hold[...]
+        kept
         + functools.reduce(jnp.add, [zdst[w].astype(jnp.float32) for w in range(nz)])
     ).astype(jnp.bfloat16)
     for copy in sends:
@@ -337,6 +346,7 @@
     rank = in_proj.shape[1]
     return (
         n_voc % PAIR == 0
+        and n_voc // PAIR > 2
         and n_tok > 1
         and (rank // ROWS16) * (tok // LANES) == n_voc
         and rank * 2 == LANES
@@ -358,7 +368,7 @@
     bf, f32 = jnp.bfloat16, jnp.float32
     block = (nz, tok, out_cols)
     dma = pltpu.SemaphoreType.DMA
-    anywhere = pl.BlockSpec(memory_space=pl.ANY)
+    anywhere = pl.BlockSpec(memory_space=pltpu.HBM)
     vmem = pl.BlockSpec(memory_space=pltpu.VMEM)
     return pl.pallas_call(
         functools.partial(fused_kernel, n_tok, n_voc, chunks),
@@ -366,14 +376,15 @@
             jax.ShapeDtypeStruct((tok, out_cols), bf),
             jax.ShapeDtypeStruct((n_tok * SPAN_DEV, store.shape[0]), f32),
         ),
-        in_specs=[anywhere] * 4 + [vmem] * 3 + [anywhere],
+        in_specs=[anywhere] * 8,
         out_specs=(vmem, vmem),
         scratch_shapes=[
             pltpu.VMEM(hidden.shape, bf),
             pltpu.VMEM(panel.shape, bf),
-            pltpu.VMEM(in_proj.shape, bf),
-            pltpu.VMEM(out_proj.shape, bf),
+            pltpu.VMEM((rank, dim), bf),
+            pltpu.VMEM((rank, cols), bf),
             pltpu.VMEM(store.shape, bf),
+            pltpu.VMEM((3, 1, tok), jnp.int32),
             pltpu.VMEM((tok, cols), f32),
             pltpu.VMEM((4, tok, LANES), f32),
             pltpu.VMEM((2 * tok, cols), bf),
@@ -389,7 +400,7 @@
             pltpu.VMEM(block, bf),
             pltpu.VMEM(block, bf),
             pltpu.VMEM(block, bf),
-            dma((4,)),
+            dma((7,)),
             dma((chunks,)),
             dma((n_voc,)),
             dma((n_voc,)),
@@ -407,13 +418,13 @@
             dma((nz,)),
         ],
         compiler_params=pltpu.CompilerParams(
-            collective_id=0, has_side_effects=True, vmem_limit_bytes=44 * 1024 * 1024
+            collective_id=0, has_side_effects=True, vmem_limit_bytes=60 * 1024 * 1024
         ),
     )(
         hidden,
         panel,
-        in_proj,
-        out_proj,
+        in_proj.T,
+        out_proj.T,
         targets.reshape(1, tok),
         keep.reshape(1, tok),
         span_ids.reshape(1, tok),

time: 48.7 us -> 39.7 us (0.82)
  local copies, waits for them, and re-layouts: 10.6 us -> 3.14 us
  Pallas kernels: 37.1 us -> 35.7 us
    unnamed x16 -> x2, local copies, waits for them, and re-layouts: 10.6 us -> 3.14 us
    pallas_call x1, Pallas kernels: 37.1 us -> 35.7 us  [body(): pl.pallas_call(functools.partial(fused_kernel, n_tok, n_voc, chunks), out...]
where the time goes in v2:
time: 39.7 us; the launch traced here: 39.5 us
  Pallas kernels  35.7 us (90%)
  local copies, waits for them, and re-layouts  3.14 us (8%)
  between operations  0.64 us (2%)
    pallas_call x1, Pallas kernels, body(): pl.pallas_call(functools.partial(fused_kernel, n_tok, n_voc, chunks), out...  35.7 us
    unnamed x2, local copies, waits for them, and re-layouts  3.14 us

profile of v2, /device:TPU:0, one launch (start us, length us, event | category | flops | bytes accessed | tf_op | source)
XLA Modules:
  0.0 39.5 jit_solution(15127806772504012203)
XLA Ops:
  0.6 35.7 %shard_map.95 = (bf16[256,256]{1,0:T(8,128)(2,1)}, f32[128,256]{1,0:T(8,128)}) custom-call(bf16[256,2048]{1,0:T(8,128)(2,1)} %hidden_hbm.1, bf16[2048,1024]{1,0:T(8,128)(2,1)} %panel_hbm.1, bf16[64,2048]{1,0:T(8,128)(2,1)} %bitcast.5, bf16[64,1024]{1,0:T(8,128)(2,1)} %bitcast.6, s32[1,256]{1,0:T(1,128)} %bitcast.7, s32[1,256]{1,0:T(1,128)} %bitcast.8, ...), custom_call_target="tpu_custom_call" | custom-call | tf_op jit(solution)/shard_map/pallas_call | solution.py:373
  36.4 1.6 %copy.12 = bf16[256,256]{1,0:T(8,128)(2,1)} copy(bf16[256,256]{1,0:T(8,128)(2,1)} %get-tuple-element.4) | data formatting | bytes 262144
  37.9 1.6 %copy.13 = f32[128,256]{1,0:T(8,128)} copy(f32[128,256]{1,0:T(8,128)} %get-tuple-element.5) | data formatting | bytes 262144

commit v3 on v2

--- a/solution.py
+++ b/solution.py
@@ -227,10 +227,14 @@
     load_outp.wait()
     outer2 = dot_nt(outp[...], both[...])
 
-    @pl.loop(0, n_voc)
-    def _(d):
-        at = pl.ds(pl.multiple_of(d * out_cols, out_cols), out_cols)
-        prod[d] = dot_nt(both[...], panel[at, :])
+    def products(side):
+        @pl.loop(0, nz)
+        def _(k):
+            d = k * PAIR + side
+            at = pl.ds(pl.multiple_of(d * out_cols, out_cols), out_cols)
+            prod[d] = dot_nt(both[...], panel[at, :])
+
+    products(PAIR - 1 - x)
 
     for k, w in enumerate(vpeers):
         remote(stat.at[v], stat.at[w], stat_s.at[k], stat_r.at[w], i, w).wait_recv()
@@ -294,6 +298,7 @@
         send(remote(oall.at[i, v], oall.at[i, v], ag_s.at[k], ag_r.at[v], i, w))
     for k in range(1, nz):
         send_x(k)
+    products(x)
     pass_on(0)
 
     for k, w in enumerate(vpeers):

time: 39.7 us -> 39.7 us (level)
  no operation moved by 1% of the time
where the time goes in v3:
time: 39.7 us; the launch traced here: 39.6 us
  Pallas kernels  35.8 us (90%)
  local copies, waits for them, and re-layouts  3.14 us (8%)
  between operations  0.64 us (2%)
    pallas_call x1, Pallas kernels, body(): pl.pallas_call(functools.partial(fused_kernel, n_tok, n_voc, chunks), out...  35.8 us
    unnamed x2, local copies, waits for them, and re-layouts  3.14 us

profile of v3, /device:TPU:0, one launch (start us, length us, event | category | flops | bytes accessed | tf_op | source)
XLA Modules:
  0.0 39.6 jit_solution(7659179709492411064)
XLA Ops:
  0.6 35.8 %shard_map.95 = (bf16[256,256]{1,0:T(8,128)(2,1)}, f32[128,256]{1,0:T(8,128)}) custom-call(bf16[256,2048]{1,0:T(8,128)(2,1)} %hidden_hbm.1, bf16[2048,1024]{1,0:T(8,128)(2,1)} %panel_hbm.1, bf16[64,2048]{1,0:T(8,128)(2,1)} %bitcast.5, bf16[64,1024]{1,0:T(8,128)(2,1)} %bitcast.6, s32[1,256]{1,0:T(1,128)} %bitcast.7, s32[1,256]{1,0:T(1,128)} %bitcast.8, ...), custom_call_target="tpu_custom_call" | custom-call | tf_op jit(solution)/shard_map/pallas_call | solution.py:378
  36.4 1.6 %copy.12 = bf16[256,256]{1,0:T(8,128)(2,1)} copy(bf16[256,256]{1,0:T(8,128)(2,1)} %get-tuple-element.4) | data formatting | bytes 262144
  38.0 1.6 %copy.13 = f32[128,256]{1,0:T(8,128)} copy(f32[128,256]{1,0:T(8,128)} %get-tuple-element.5) | data formatting | bytes 262144

commit v4 on v2

--- a/solution.py
+++ b/solution.py
@@ -76,9 +76,7 @@
     panel_hbm,
     inp_hbm,
     outp_hbm,
-    targets_hbm,
-    keep_hbm,
-    span_hbm,
+    ids_hbm,
     store_hbm,
     hg_ref,
     scores_ref,
@@ -150,10 +148,8 @@
         pl.semaphore_signal(barrier, inc=1, device_id=(t, v), device_id_type=MESH_ID)
 
     width = cols // chunks
-    loads = []
-    for k, ref in enumerate((targets_hbm, keep_hbm, span_hbm)):
-        loads.append(pltpu.make_async_copy(ref, ids_ref.at[k], load_sem.at[4 + k]))
-        loads[-1].start()
+    load_ids = pltpu.make_async_copy(ids_hbm, ids_ref, load_sem.at[4])
+    load_ids.start()
     load_hidden = pltpu.make_async_copy(hidden_hbm, hidden, load_sem.at[0])
     load_hidden.start()
     load_inp = pltpu.make_async_copy(inp_hbm, inp, load_sem.at[1])
@@ -170,8 +166,7 @@
     load_store = pltpu.make_async_copy(store_hbm, store, load_sem.at[3])
     load_store.start()
 
-    for copy in loads:
-        copy.wait()
+    load_ids.wait()
     target_col = jnp.broadcast_to(ids_ref[0].astype(jnp.float32), (LANES, tok)).T
     keep_row = ids_ref[1].astype(jnp.float32)
     keep_col = jnp.broadcast_to(keep_row, (LANES, tok)).T
@@ -376,7 +371,7 @@
             jax.ShapeDtypeStruct((tok, out_cols), bf),
             jax.ShapeDtypeStruct((n_tok * SPAN_DEV, store.shape[0]), f32),
         ),
-        in_specs=[anywhere] * 8,
+        in_specs=[anywhere] * 6,
         out_specs=(vmem, vmem),
         scratch_shapes=[
             pltpu.VMEM(hidden.shape, bf),
@@ -400,7 +395,7 @@
             pltpu.VMEM(block, bf),
             pltpu.VMEM(block, bf),
             pltpu.VMEM(block, bf),
-            dma((7,)),
+            dma((5,)),
             dma((chunks,)),
             dma((n_voc,)),
             dma((n_voc,)),
@@ -418,16 +413,14 @@
             dma((nz,)),
         ],
         compiler_params=pltpu.CompilerParams(
-            collective_id=0, has_side_effects=True, vmem_limit_bytes=60 * 1024 * 1024
+            collective_id=0, has_side_effects=True, vmem_limit_bytes=54900 * 1024
         ),
     )(
         hidden,
         panel,
         in_proj.T,
         out_proj.T,
-        targets.reshape(1, tok),
-        keep.reshape(1, tok),
-        span_ids.reshape(1, tok),
+        jnp.stack([targets, keep, span_ids]).reshape(3, 1, tok),
         store,
     )
 

time: 39.7 us -> 37.5 us (0.945)
  local copies, waits for them, and re-layouts: 3.14 us -> 1.32 us
  Pallas kernels: 35.7 us -> 34.6 us
  other arithmetic: 0 us -> 0.72 us
    unnamed x2, local copies, waits for them, and re-layouts: 3.14 us -> 1.31 us
    pallas_call x1, Pallas kernels: 35.7 us -> 34.6 us  [body(): pl.pallas_call(functools.partial(fused_kernel, n_tok, n_voc, chunks), out...]
    another operation x0 -> x1, other arithmetic: none -> 0.72 us  [body(): jnp.stack([targets, keep, span_ids]).reshape(3, 1, tok)]
where the time goes in v4:
time: 37.5 us; the launch traced here: 37.3 us
  Pallas kernels  34.6 us (92%)
  local copies, waits for them, and re-layouts  1.32 us (4%)
  other arithmetic  0.72 us (2%)
  between operations  0.64 us (2%)
    pallas_call x1, Pallas kernels, body(): pl.pallas_call(functools.partial(fused_kernel, n_tok, n_voc, chunks), out...  34.6 us
    unnamed x2, local copies, waits for them, and re-layouts  1.31 us

profile of v4, /device:TPU:0, one launch (start us, length us, event | category | flops | bytes accessed | tf_op | source)
XLA Modules:
  0.0 37.3 jit_solution(8572323240839389938)
XLA Ops:
  0.6 0.7 %pad_add_fusion = s32[3,256]{1,0:T(4,128)S(1)} fusion(s32[1,256]{1,0:T(1,128)} %bitcast.7, s32[1,256]{1,0:T(1,128)} %bitcast.8, s32[1,256]{1,0:T(1,128)} %bitcast.9), kind=kLoop, calls=%fused_computation | loop fusion | flops 1536 | bytes 6144 | tf_op jit(solution)/shard_map/stack | solution.py:423
  1.4 34.6 %shard_map.95 = (bf16[256,256]{1,0:T(8,128)(2,1)S(1)}, f32[128,256]{1,0:T(8,128)S(1)}) custom-call(bf16[256,2048]{1,0:T(8,128)(2,1)} %hidden_hbm.1, bf16[2048,1024]{1,0:T(8,128)(2,1)} %panel_hbm.1, bf16[64,2048]{1,0:T(8,128)(2,1)} %bitcast.5, bf16[64,1024]{1,0:T(8,128)(2,1)} %bitcast.6, s32[3,1,256]{2,1,0:T(1,128)S(1)} %reshape.7.ids_hbm, ...), custom_call_target="tpu_custom_call" | custom-call | tf_op jit(solution)/shard_map/pallas_call | solution.py:368
  36.0 0.7 %copy.12 = bf16[256,256]{1,0:T(8,128)(2,1)} copy(bf16[256,256]{1,0:T(8,128)(2,1)S(1)} %get-tuple-element.4) | data formatting | bytes 262144
  36.7 0.7 %copy.13 = f32[128,256]{1,0:T(8,128)} copy(f32[128,256]{1,0:T(8,128)S(1)} %get-tuple-element.5) | data formatting | bytes 262144
  (1 shorter events, 0.0 us)
